TPU v7x, 256 devices: a whole 4x4x8 slice. The times are simulated.
256 devices in a mesh: dp: 2 (over core), seq: 128 (over z, y, x).
Axes of the slice: x: 4, y: 4, z: 8, core: 2. Of those that a mesh axis runs over, the one named last changes fastest.
Arguments:
- query_tiles: bfloat16 [2, 128, 2, 64, 4096], P('dp', 'seq'), may hold values from -6 to 6
- key_tiles: bfloat16 [2, 128, 2, 64, 4096], P('dp', 'seq'), may hold values from -6 to 6
- value_tiles: bfloat16 [2, 128, 2, 64, 4096], P('dp', 'seq'), may hold values from -6 to 6
- cotangent: bfloat16 [2, 16384, 4096], P('dp', 'seq'), may hold values from -6 to 6
- filters: bfloat16 [128, 128], replicated, may hold values from -0.5 to 0.5
- doc_lengths: int32 [2, 8], replicated, may hold values from 1 to 8192, 16384 in all within a row
- arrival: int32 [2, 128, 2], P(None, 'seq'), may hold values from 0 to 1, as said below
Outputs:
- grad_query: bfloat16 [2, 128, 2, 64, 4096], P('dp', 'seq')
- grad_key: bfloat16 [2, 128, 2, 64, 4096], P('dp', 'seq')
- grad_value: bfloat16 [2, 128, 2, 64, 4096], P('dp', 'seq')
- grad_filters: float32 [128, 128], replicated
Inputs may be any that keep to these rules, and one draw needn't show every extreme that they name: For every block s and sequence j, arrival[d, s, j] over all d is a permutation of 0 to 1.
All inputs are finite; a program needn't handle non-finite values.
Results may differ from a plain program's by a relative error of at most 0.005.
Values may be sent and summed in bfloat16 or wider, within the bound.
A program may use at most 192 MiB of HBM per device.

v0:
```python
import math

import jax
import jax.numpy as jnp
from jax import lax
from jax.sharding import PartitionSpec as P


def passed_along(array, axis, by):
    count = lax.axis_size(axis)
    pairs = [(i, i + by) for i in range(count) if 0 <= i + by < count]
    return lax.ppermute(array, axis, pairs)


def doc_starts(positions, doc_lens, doc_ends):
    return jnp.sum(jnp.where(positions[:, None] >= doc_ends[None, :], doc_lens[None, :], 0), axis=1)


def forward_base(filters, block_rows, kernel):
    span = block_rows + kernel
    group_count = filters.shape[0]
    pattern = jnp.concatenate(
        [
            jnp.zeros((group_count, 1), filters.dtype),
            filters[:, ::-1],
            jnp.zeros((group_count, span - kernel), filters.dtype),
        ],
        axis=1,
    )
    tiled = jnp.broadcast_to(pattern[:, None, :], (group_count, block_rows, span + 1)).reshape(
        group_count, block_rows * (span + 1)
    )
    return tiled[:, : block_rows * span].reshape(group_count, block_rows, span)


def backward_base(filters, block_rows, kernel):
    span = block_rows + kernel
    group_count = filters.shape[0]
    pattern = jnp.concatenate(
        [filters, jnp.zeros((group_count, span + 1 - kernel), filters.dtype)], axis=1
    )
    tiled = jnp.broadcast_to(pattern[:, None, :], (group_count, block_rows, span + 1)).reshape(
        group_count, block_rows * (span + 1)
    )
    return tiled[:, : block_rows * span].reshape(group_count, block_rows, span)


def forward_block(
    extended, gate_grad, start_row, block_rows, base_fwd, first_pos, doc_lens, doc_ends, kernel
):
    group_count = base_fwd.shape[0]
    span = block_rows + kernel
    window = extended[start_row : start_row + span]
    rows_pos = first_pos + start_row + jnp.arange(block_rows, dtype=jnp.int32)
    left_pos = first_pos + start_row - kernel + jnp.arange(span, dtype=jnp.int32)
    inside = left_pos[None, :] >= doc_starts(rows_pos, doc_lens, doc_ends)[:, None]
    matrix = base_fwd * inside.astype(jnp.bfloat16)[None]
    features = window.reshape(span, group_count, -1)
    hidden = jnp.einsum(
        "gte,egc->tgc", matrix, features, preferred_element_type=jnp.float32
    ).reshape(block_rows, -1)
    gradient = gate_grad[start_row : start_row + block_rows].reshape(block_rows, group_count, -1)
    correl = (
        jnp.einsum("tgc,egc->gte", gradient, features, preferred_element_type=jnp.float32)
        * inside.astype(jnp.float32)[None]
    )
    skewed = jnp.pad(
        correl.reshape(group_count, block_rows * span), ((0, 0), (0, block_rows))
    ).reshape(group_count, block_rows, span + 1)
    filter_terms = jnp.sum(skewed[:, :, 1 : kernel + 1], axis=1)[:, ::-1]
    return (hidden, filter_terms)


def backward_block(
    extended, start_row, block_rows, base_back, first_pos, doc_lens, doc_ends, kernel
):
    group_count = base_back.shape[0]
    span = block_rows + kernel
    window = extended[start_row : start_row + span]
    rows_pos = first_pos + start_row + jnp.arange(block_rows, dtype=jnp.int32)
    right_pos = first_pos + start_row + jnp.arange(span, dtype=jnp.int32)
    inside = rows_pos[:, None] >= doc_starts(right_pos, doc_lens, doc_ends)[None, :]
    matrix = base_back * inside.astype(jnp.bfloat16)[None]
    features = window.reshape(span, group_count, -1)
    return jnp.einsum("gpt,tgc->pgc", matrix, features, preferred_element_type=jnp.float32).reshape(
        block_rows, -1
    )


def body(query_tiles, key_tiles, value_tiles, cotangent, filters, doc_lengths, arrival):
    dp_count = lax.axis_size("dp")
    seq_count = lax.axis_size("seq")
    slot_rows = query_tiles.shape[3]
    feature_count = query_tiles.shape[4]
    group_count, kernel = filters.shape
    group_size = feature_count // group_count
    local_rows = dp_count * slot_rows
    block_rows = min(local_rows, max(16, local_rows // 8))
    sequence = lax.axis_index("dp")
    shard_index = lax.axis_index("seq")
    first_pos = shard_index * local_rows
    doc_lens = lax.dynamic_slice_in_dim(doc_lengths, sequence, 1, 0)[0]
    doc_ends = jnp.cumsum(doc_lens)
    held_tiles = lax.dynamic_slice_in_dim(arrival[:, 0, :], sequence, 1, 1)[:, 0]
    placer = held_tiles[None, :] == jnp.arange(dp_count, dtype=jnp.int32)[:, None]
    placer_half = placer.astype(jnp.bfloat16)

    def arrange(tiles):
        ordered = jnp.einsum("td,drc->trc", placer_half, tiles, preferred_element_type=jnp.float32)
        return ordered.astype(jnp.bfloat16).reshape(local_rows, feature_count)

    def restore_half(logical):
        tiles = logical.reshape(dp_count, slot_rows, feature_count)
        return jnp.einsum(
            "td,trc->drc", placer_half, tiles, preferred_element_type=jnp.float32
        ).astype(jnp.bfloat16)

    query_home = query_tiles.reshape(dp_count, slot_rows, feature_count)
    key_home = key_tiles.reshape(dp_count, slot_rows, feature_count)
    value_home = value_tiles.reshape(dp_count, slot_rows, feature_count)
    grad_rows = cotangent[0].astype(jnp.float32)
    query_in, key_in, value_in = (
        lax.all_to_all(query_home, "dp", split_axis=0, concat_axis=0, tiled=True),
        lax.all_to_all(key_home, "dp", split_axis=0, concat_axis=0, tiled=True),
        lax.all_to_all(value_home, "dp", split_axis=0, concat_axis=0, tiled=True),
    )
    queries = arrange(query_in)
    keys_seq = arrange(key_in)
    values_seq = arrange(value_in)
    mixture = (keys_seq.astype(jnp.float32) * values_seq.astype(jnp.float32)).astype(jnp.bfloat16)
    gate_grad = (grad_rows * queries.astype(jnp.float32)).astype(jnp.bfloat16)
    previous = passed_along(mixture[local_rows - (kernel - 1) :], "seq", 1)
    extended = jnp.concatenate(
        [jnp.zeros((1, feature_count), jnp.bfloat16), previous, mixture], axis=0
    )
    base_fwd = forward_base(filters, block_rows, kernel)
    base_back = backward_base(filters, block_rows, kernel)
    hidden_list = []
    filter_terms = jnp.zeros((group_count, kernel), jnp.float32)
    for start_row in range(0, local_rows, block_rows):
        hidden_part, terms = forward_block(
            extended,
            gate_grad,
            start_row,
            block_rows,
            base_fwd,
            first_pos,
            doc_lens,
            doc_ends,
            kernel,
        )
        hidden_list.append(hidden_part)
        filter_terms = filter_terms + terms
    hidden = jnp.concatenate(hidden_list, axis=0)
    trailing = passed_along(gate_grad[: kernel - 1], "seq", -1)
    grad_ext = jnp.concatenate(
        [gate_grad, trailing, jnp.zeros((1, feature_count), jnp.bfloat16)], axis=0
    )
    mix_grad = jnp.concatenate(
        [
            backward_block(
                grad_ext, start_row, block_rows, base_back, first_pos, doc_lens, doc_ends, kernel
            )
            for start_row in range(0, local_rows, block_rows)
        ],
        axis=0,
    )
    grad_q_seq = (grad_rows * hidden).astype(jnp.bfloat16)
    grad_k_seq = (mix_grad * values_seq.astype(jnp.float32)).astype(jnp.bfloat16)
    grad_v_seq = (mix_grad * keys_seq.astype(jnp.float32)).astype(jnp.bfloat16)
    grad_q_home, grad_k_home, grad_v_home = (
        lax.all_to_all(restore_half(grad_q_seq), "dp", split_axis=0, concat_axis=0, tiled=True),
        lax.all_to_all(restore_half(grad_k_seq), "dp", split_axis=0, concat_axis=0, tiled=True),
        lax.all_to_all(restore_half(grad_v_seq), "dp", split_axis=0, concat_axis=0, tiled=True),
    )
    total_terms = lax.psum(filter_terms, ("dp", "seq"))
    grad_filters = total_terms * (1.0 / math.sqrt(dp_count * local_rows * seq_count * group_size))
    out_shape = query_tiles.shape
    return (
        grad_q_home.reshape(out_shape),
        grad_k_home.reshape(out_shape),
        grad_v_home.reshape(out_shape),
        grad_filters,
    )


def solution(mesh):
    placed = (
        P("dp", "seq", None, None, None),
        P("dp", "seq", None, None, None),
        P("dp", "seq", None, None, None),
        P("dp", "seq", None),
        P(),
        P(),
        P(None, "seq", None),
    )
    return jax.shard_map(
        body,
        mesh=mesh,
        in_specs=placed,
        out_specs=(
            P("dp", "seq", None, None, None),
            P("dp", "seq", None, None, None),
            P("dp", "seq", None, None, None),
            P(),
        ),
        check_vma=False,
    )
```

profile of v0, /device:TPU:1, one launch (start us, length us, event | category | flops | bytes accessed | tf_op | source)
XLA Modules:
  0.0 522.8 jit_solution(12939483965062244811)
XLA Ops:
  7.2 6.8 %all-to-all-start.1 = ((bf16[2,64,4096]{2,1,0:T(8,128)(2,1)}), bf16[2,64,4096]{2,1,0:T(8,128)(2,1)S(1)}, u32[]{:S(2)}, u32[]{:S(2)}) async-start(bf16[2,64,4096]{2,1,0:T(8,128)(2,1)} %bitcast.196), calls=%async_computation.1 | async-start | bytes 2097152 | tf_op jit(solution)/shard_map/all_to_all | solution.py:125
  15.8 3.9 all-to-all-start
  19.7 2.9 fusion.1
  22.6 5.0 multiply_convert_fusion.3
  31.7 4.5 all_to_all.30
  63.0 4.7 broadcast_multiply_fusion
  103.1 4.5 broadcast_multiply_fusion.8
  127.3 5.9 %pad_maximum_fusion.3 = (bf16[144,4096]{1,0:T(8,128)(2,1)}, bf16[144,4096]{1,0:T(8,128)(2,1)}, bf16[144,4096]{1,0:T(8,128)(2,1)}, bf16[144,4096]{1,0:T(8,128)(2,...) fusion(bf16[128,4096]{1,0:T(8,128)(2,1)S(1)} %bitcast.172, ...), kind=kLoop, calls=%fused_computation.78 | loop fusion | flops 20054016 | bytes 11534336 | tf_op jit(solution)/shard_map/concatenate | solution.py:133
  133.2 3.5 copy.196
  136.7 3.0 convolution_multiply_fusion.7
  148.6 3.7 copy.200
  152.3 3.7 convolution_multiply_fusion.6
  165.0 3.7 copy.203
  168.7 3.7 convolution_multiply_fusion.5
  181.4 3.6 copy.206
  185.1 3.6 convolution_multiply_fusion.4
  197.7 3.7 copy.209
  201.3 3.7 convolution_multiply_fusion.3
  214.0 3.7 copy.212
  217.6 3.6 convolution_multiply_fusion.2
  228.8 3.7 copy.215
  232.4 3.8 convolution_multiply_fusion.1
  248.7 3.7 copy.218
  252.4 3.5 convolution_multiply_fusion
  256.0 2.8 copy.270
  268.6 6.1 %pad_maximum_fusion = (bf16[144,4096]{1,0:T(8,128)(2,1)}, bf16[144,4096]{1,0:T(8,128)(2,1)}, bf16[144,4096]{1,0:T(8,128)(2,1)}, bf16[144,4096]{1,0:T(8,128)(2,1)...) fusion(bf16[1,4096]{1,0:T(2,128)(2,1)} %copy-done.31, ...), kind=kLoop, calls=%fused_computation.75 | loop fusion | flops 20054016 | bytes 11534336 | tf_op jit(solution)/shard_map/concatenate | solution.py:156
  274.7 3.7 copy.226
  350.4 5.0 convolution_convert_fusion.1
  359.2 4.8 all-to-all-start.5
  396.1 4.2 all_to_all.31
  400.9 4.6 all_to_all.32
  405.5 104.3 %all-reduce.11.cloned.1.call-done = f32[128,128]{0,1:T(8,128)} async-done(((f32[128,128]{0,1:T(8,128)}), f32[128,128]{0,1:T(8,128)}) %all-reduce.11.cloned.1.call-update) | async-done | bytes 65552 | tf_op jit(solution)/shard_map/psum | solution.py:176
  (321 shorter events, 276.1 us)
Async XLA Ops:
  7.2 6.8 %copy-start = (s32[2,1,2]{2,1,0:T(1,128)S(1)}, s32[2,1,2]{2,1,0:T(1,128)}, u32[]{:S(2)}) copy-start(s32[2,1,2]{2,1,0:T(1,128)} %param.13) | copy-start | bytes 52
  7.2 8.6 %all-to-all-start.1 = ((bf16[2,64,4096]{2,1,0:T(8,128)(2,1)}), bf16[2,64,4096]{2,1,0:T(8,128)(2,1)S(1)}, u32[]{:S(2)}, u32[]{:S(2)}) async-start(bf16[2,64,4096]{2,1,0:T(8,128)(2,1)} %bitcast.196), calls=%async_computation.1 | async-start | bytes 2097152 | tf_op jit(solution)/shard_map/all_to_all | solution.py:125
  14.2 22.1 %copy-start.49 = (s32[2]{0:T(128)}, s32[2]{0:T(128)S(1)}, u32[]{:S(2)}) copy-start(s32[2]{0:T(128)S(1)} %dynamic-slice_reduce_fusion) | copy-start | bytes 28
  15.8 6.8 %all-to-all-start = ((bf16[2,64,4096]{2,1,0:T(8,128)(2,1)}), bf16[2,64,4096]{2,1,0:T(8,128)(2,1)S(1)}, u32[]{:S(2)}, u32[]{:S(2)}) async-start(bf16[2,64,4096]{2,1,0:T(8,128)(2,1)} %bitcast.3), calls=%async_computation | async-start | bytes 2097152 | tf_op jit(solution)/shard_map/all_to_all | solution.py:124
  19.7 490.1 %all-reduce.11.cloned.1.call-start = ((), (), s32[]{:S(2)}) async-start(), calls=%async_computation.6 | async-start | bytes 131072 | tf_op jit(solution)/shard_map/psum | solution.py:176
  27.5 4.2 copy-start.28
  29.4 98.0 %collective-permute-start = (bf16[127,4096]{1,0:T(8,128)(2,1)}, bf16[127,4096]{1,0:T(8,128)(2,1)}, u32[]{:S(2)}, u32[]{:S(2)}) collective-permute-start(bf16[127,4096]{1,0:T(8,128)(2,1)} %slice.158), channel_id=1, source_target_pairs={{0,1},{1,2},{2,3},{3,4},{4,5},{5,6},{6,7},{7,8},{8,9},{9,10},{10,1... | collective-permute-start | bytes 3121160 | tf_op jit(solution)/shard_map/ppermute | solution.py:12
  39.7 9.5 %copy-start.32 = (bf16[128,128]{1,0:T(8,128)(2,1)S(1)}, bf16[128,128]{1,0:T(8,128)(2,1)}, u32[]{:S(2)}) copy-start(bf16[128,128]{1,0:T(8,128)(2,1)} %param.11) | copy-start | bytes 98308
  39.7 9.7 %copy-start.51 = (s32[2,8]{1,0:T(2,128)S(1)}, s32[2,8]{1,0:T(2,128)}, u32[]{:S(2)}) copy-start(s32[2,8]{1,0:T(2,128)} %param.12) | copy-start | bytes 196
  39.7 228.9 %collective-permute-start.1 = (bf16[127,4096]{1,0:T(8,128)(2,1)S(1)}, bf16[127,4096]{1,0:T(8,128)(2,1)}, u32[]{:S(2)}, u32[]{:S(2)}) collective-permute-start(bf16[127,4096]{1,0:T(8,128)(2,1)S(1)} %bitcast.173), channel_id=1, source_target_pairs={{1,0},{2,1},{3,2},{4,3},{5,4},{6,5},{7,6},{8,7},{9,8},{10,9},{11,1... | collective-permute-start | bytes 3121160 | tf_op jit(solution)/shard_map/ppermute | solution.py:12
  42.4 14.9 %copy-start.40 = (s32[16]{0:T(128)}, s32[16]{0:T(128)S(1)}, u32[]{:S(2)}) copy-start(s32[16]{0:T(128)S(1)} %iota_add_fusion.16) | copy-start | bytes 196
  43.0 14.3 %copy-start.41 = (s32[16]{0:T(128)}, s32[16]{0:T(128)S(1)}, u32[]{:S(2)}) copy-start(s32[16]{0:T(128)S(1)} %iota_add_fusion.17) | copy-start | bytes 196
  43.5 13.8 %copy-start.42 = (s32[16]{0:T(128)}, s32[16]{0:T(128)S(1)}, u32[]{:S(2)}) copy-start(s32[16]{0:T(128)S(1)} %iota_add_fusion.18) | copy-start | bytes 196
  92.4 6.9 %copy-start.30 = (bf16[128,145]{1,0:T(8,128)(2,1)S(1)}, bf16[128,145]{1,0:T(8,128)(2,1)}, u32[]{:S(2)}) copy-start(bf16[128,145]{1,0:T(8,128)(2,1)} %maximum_maximum_fusion) | copy-start | bytes 111364
  97.6 4.1 copy-start.47
  97.6 4.1 copy-start.37
  97.6 4.1 copy-start.44
  97.6 4.1 copy-start.46
  97.6 4.8 copy-start.43
  97.6 4.8 copy-start.48
  127.3 5.9 %copy-start.31 = (bf16[1,4096]{1,0:T(2,128)(2,1)}, bf16[1,4096]{1,0:T(2,128)(2,1)S(1)}, u32[]{:S(2)}) copy-start(bf16[1,4096]{1,0:T(2,128)(2,1)S(1)} %broadcast.543) | copy-start | bytes 24580
  147.2 5.1 copy-start.33
  342.2 6.0 %copy-start.22 = (f32[16,4096]{1,0:T(8,128)S(1)}, f32[16,4096]{1,0:T(8,128)}, u32[]{:S(2)}) copy-start(f32[16,4096]{1,0:T(8,128)} %reshape.1028) | copy-start | bytes 786436
  342.2 6.7 %copy-start.24 = (f32[16,4096]{1,0:T(8,128)S(1)}, f32[16,4096]{1,0:T(8,128)}, u32[]{:S(2)}) copy-start(f32[16,4096]{1,0:T(8,128)} %reshape.1030) | copy-start | bytes 786436
  342.2 7.5 %copy-start.26 = (f32[16,4096]{1,0:T(8,128)S(1)}, f32[16,4096]{1,0:T(8,128)}, u32[]{:S(2)}) copy-start(f32[16,4096]{1,0:T(8,128)} %reshape.1032) | copy-start | bytes 786436
  342.2 8.2 %copy-start.50 = (s32[2]{0:T(128)S(1)}, s32[2]{0:T(128)}, u32[]{:S(2)}) copy-start(s32[2]{0:T(128)} %copy-done.49) | copy-start | bytes 28
  342.2 8.2 %copy-start.52 = (f32[2,64,4096]{2,0,1:T(2,128)S(1)}, f32[2,64,4096]{2,0,1:T(2,128)}, u32[]{:S(2)}) copy-start(f32[2,64,4096]{2,0,1:T(2,128)} %fusion.1) | copy-start | bytes 6291460
  350.4 5.0 copy-start.36
  350.4 5.0 copy-start.53
  357.6 6.3 %copy-start.17 = (bf16[128,16,144]{2,1,0:T(8,128)(2,1)S(1)}, bf16[128,16,144]{2,1,0:T(8,128)(2,1)}, u32[]{:S(2)}) copy-start(bf16[128,16,144]{2,1,0:T(8,128)(2,1)} %copy.198) | copy-start | bytes 1769476
  359.2 36.3 %all-to-all-start.5 = ((bf16[2,64,4096]{2,1,0:T(8,128)(2,1)}), bf16[2,64,4096]{2,1,0:T(8,128)(2,1)}, u32[]{:S(2)}, u32[]{:S(2)}) async-start(bf16[2,64,4096]{2,1,0:T(8,128)(2,1)} %copy.254), calls=%async_computation.5 | async-start | bytes 2097152 | tf_op jit(solution)/shard_map/all_to_all | solution.py:174
  511.4 4.2 copy-start.1
  (28 other events, 80.4 us)
Sparse Core Ops, SparseCore 0:
  268.7 241.0 all-reduce.10
where the time goes:
time: 532 us; the launch traced here: 523 us
  local copies, waits for them, and re-layouts  233 us (44%)
  waiting for transfers between devices  106 us (20%)
  matrix products  80.3 us (15%)
  other arithmetic  56.3 us (11%)
  starting transfers between devices  19.2 us (4%)
  between operations  15.3 us (3%)
  blocking collectives  13.4 us (3%)
    psum x1, waiting for transfers between devices, body(): total_terms = lax.psum(filter_terms, ('dp', 'seq'))  104 us
    slice x8, local copies, waits for them, and re-layouts, forward_block(): window = extended[start_row:start_row + span]  29.1 us
    dot_general x8, matrix products, forward_block(): jnp.einsum('tgc,egc->gte', gradient, features, preferred_element_type=jnp...  28.6 us
    mul x8, local copies, waits for them, and re-layouts, forward_block(): jnp.einsum('tgc,egc->gte', gradient, features, preferred_element_type=jnp...  22.2 us
    slice x8, local copies, waits for them, and re-layouts, backward_block(): window = extended[start_row:start_row + span]  20.7 us
    mul x8, local copies, waits for them, and re-layouts, backward_block(): matrix = base_back * inside.astype(jnp.bfloat16)[None]  19.7 us
    dot_general x8, matrix products, backward_block(): jnp.einsum('gpt,tgc->pgc', matrix, features, preferred_element_type=jnp.f...  19.7 us
    mul x8, local copies, waits for them, and re-layouts, forward_block(): matrix = base_fwd * inside.astype(jnp.bfloat16)[None]  19.7 us
  transfers between devices with their start and end apart: 6, of which 2 were waited for; matrix products, arithmetic and copies ran while one was open for 68% of the time, Pallas kernels for 0%

commit v1 on v0

v1 whole, which is shorter than its diff:
```python
import functools
import math

import jax
import jax.numpy as jnp
from jax import lax
from jax.experimental import pallas as pl
from jax.experimental.pallas import tpu as pltpu
from jax.sharding import PartitionSpec as P

MESH = pl.DeviceIdType.MESH
LANES = 128


def kernel_body(
    dims,
    chunks,
    inflight,
    scale,
    query_hbm,
    key_hbm,
    value_hbm,
    cot_hbm,
    filters_ref,
    doc_ref,
    arrival_ref,
    gq_hbm,
    gk_hbm,
    gv_hbm,
    gf_hbm,
    own,
    rcv,
    cot,
    mixx,
    ggx,
    taps_fwd,
    taps_back,
    rolled_fwd,
    rolled_back,
    masks_half,
    masks,
    diag,
    terms,
    stage_own,
    stage_oth,
    piece_one,
    piece_two,
    piece_three,
    own_sem,
    cot_sem,
    swap_send,
    swap_recv,
    mix_send,
    mix_recv,
    gg_send,
    gg_recv,
    out_sem,
    back_send,
    back_recv,
    one_send,
    one_recv,
    two_send,
    two_recv,
    three_send,
    three_recv,
    four_send,
    four_recv,
    final_sem,
):
    z_count, y_count, x_count = dims
    seq_count = z_count * y_count * x_count
    group_count, kernel = filters_ref.shape
    rows = kernel
    slot = own.shape[2]
    width = own.shape[3]
    tile_count = mixx.shape[0]
    per_chunk = tile_count // chunks
    per_tile = group_count // tile_count
    group_size = LANES // per_tile
    half_chunks = chunks // 2
    core = lax.axis_index("dp")
    other = 1 - core
    seq = lax.axis_index("seq")
    x = lax.rem(seq, x_count)
    y = lax.rem(lax.div(seq, x_count), y_count)
    z = lax.div(seq, x_count * y_count)
    sibling = (other, seq)
    following = (core, lax.rem(seq + 1, seq_count))
    previous = (core, lax.rem(seq + seq_count - 1, seq_count))
    team = 2 * x_count
    place = core * x_count + x

    def member(k):
        index = lax.rem(place + k, team)
        return index, (lax.div(index, x_count), seq - x + lax.rem(index, x_count))

    def along_y(k):
        index = lax.rem(y + k, y_count)
        return index, (core, seq + (index - y) * x_count)

    def along_z(k):
        index = lax.rem(z + k, z_count)
        return index, (core, seq + (index - z) * (x_count * y_count))

    def columns(c):
        return pl.ds(pl.multiple_of(c * width, width), width)

    sources = (key_hbm, value_hbm, query_hbm)

    def chunk_of(which, c):
        return chunks - 1 - c if which == 2 else c

    def own_copy(which, c):
        return pltpu.make_async_copy(
            sources[which].at[0, 0, core, :, columns(c)],
            own.at[which, c],
            own_sem.at[which, c],
        )

    def cot_copy(c):
        return pltpu.make_async_copy(cot_hbm.at[0, :, columns(c)], cot.at[c], cot_sem.at[c])

    def swap_copy(which, c):
        return pltpu.make_async_remote_copy(
            src_ref=sources[which].at[0, 0, other, :, columns(c)],
            dst_ref=rcv.at[which, c],
            send_sem=swap_send.at[which, c],
            recv_sem=swap_recv.at[which, c],
            device_id=sibling,
            device_id_type=MESH,
        )

    for c in range(chunks):
        for which in range(3):
            own_copy(which, chunk_of(which, c)).start()
        cot_copy(chunks - 1 - c).start()

    barrier = pltpu.get_barrier_semaphore()
    partners = [sibling, following, previous]
    partners += [member(k)[1] for k in range(1, team)]
    partners += [along_y(k)[1] for k in range(1, y_count)]
    partners += [along_z(k)[1] for k in range(1, z_count)]
    for partner in partners:
        pl.semaphore_signal(barrier, inc=1, device_id=partner, device_id_type=MESH)

    square = (rows, rows)
    row = lax.broadcasted_iota(jnp.int32, square, 0)
    col = lax.broadcasted_iota(jnp.int32, square, 1)
    first = seq * rows

    def doc_start(position):
        end = jnp.int32(0)
        result = jnp.zeros(square, jnp.int32)
        for i in range(doc_ref.shape[1]):
            length = doc_ref[core, i]
            end = end + length
            result = result + jnp.where(position >= end, length, 0)
        return result

    def as_mask(condition):
        return jnp.where(condition, 1.0, 0.0).astype(jnp.float32)

    start_row = doc_start(first + row)
    start_col = doc_start(first + col)
    start_far = doc_start(first + rows + col)
    built = (
        as_mask((col > row) & (first - rows + col >= start_row)),
        as_mask((col <= row) & (first + col >= start_row)),
        as_mask((col >= row) & (first + row >= start_col)),
        as_mask((col < row) & (first + row >= start_far)),
    )
    for i, mask in enumerate(built):
        masks[i] = mask
        masks_half[i] = mask.astype(jnp.bfloat16)

    flip = as_mask(lax.rem(row + col, kernel) == 0)

    pl.semaphore_wait(barrier, len(partners))
    for c in range(chunks):
        for which in range(3):
            swap_copy(which, chunk_of(which, c)).start()

    straight = filters_ref[...].astype(jnp.float32)
    turned = jnp.dot(
        filters_ref[...], flip.astype(jnp.bfloat16), preferred_element_type=jnp.float32
    )
    for s in range(8):
        rolled_fwd[pl.ds(s, group_count, stride=8), :] = pltpu.roll(turned, s, 1)
        rolled_back[pl.ds(s, group_count, stride=8), :] = pltpu.roll(straight, s, 1)

    held = arrival_ref[core, 0, core]
    own_first = jnp.full((slot, LANES), held, jnp.int32) == 0

    def in_order(mine, received):
        return jnp.concatenate(
            [jnp.where(own_first, mine, received), jnp.where(own_first, received, mine)], axis=0
        )

    def halo_mix(c):
        tiles = pl.ds(c * per_chunk, per_chunk)
        return pltpu.make_async_remote_copy(
            src_ref=mixx.at[tiles, pl.ds(rows, rows), :],
            dst_ref=mixx.at[tiles, pl.ds(0, rows), :],
            send_sem=mix_send.at[c],
            recv_sem=mix_recv.at[c],
            device_id=following,
            device_id_type=MESH,
        )

    def halo_gg(c):
        tiles = pl.ds(c * per_chunk, per_chunk)
        return pltpu.make_async_remote_copy(
            src_ref=ggx.at[tiles, pl.ds(0, rows), :],
            dst_ref=ggx.at[tiles, pl.ds(rows, rows), :],
            send_sem=gg_send.at[c],
            recv_sem=gg_recv.at[c],
            device_id=previous,
            device_id_type=MESH,
        )

    def assemble(c, carry):
        back = chunks - 1 - c
        for which in range(2):
            own_copy(which, c).wait()
            swap_copy(which, c).wait_recv()
        for q in range(per_chunk):
            lanes = slice(q * LANES, (q + 1) * LANES)
            mine = own[0, c, :, lanes].astype(jnp.float32) * own[1, c, :, lanes].astype(jnp.float32)
            received = rcv[0, c, :, lanes].astype(jnp.float32) * rcv[1, c, :, lanes].astype(
                jnp.float32
            )
            mixx[c * per_chunk + q, rows:, :] = in_order(mine, received).astype(jnp.bfloat16)

        @pl.when(c < inflight)
        def _():
            halo_mix(c).start()

        own_copy(2, back).wait()
        swap_copy(2, back).wait_recv()
        cot_copy(back).wait()
        for q in range(per_chunk):
            lanes = slice(q * LANES, (q + 1) * LANES)
            gate = in_order(
                own[2, back, :, lanes].astype(jnp.float32),
                rcv[2, back, :, lanes].astype(jnp.float32),
            )
            ggx[back * per_chunk + q, :rows, :] = (
                gate * cot[back, :, lanes].astype(jnp.float32)
            ).astype(jnp.bfloat16)

        @pl.when(c < inflight)
        def _():
            halo_gg(back).start()

        return carry

    lax.fori_loop(0, chunks, assemble, 0)

    def band(g, carry):
        base = pl.multiple_of(g * rows, rows)
        eight = pl.ds(pl.multiple_of(g * 8, 8), 8)
        for rolled, out, near, far in (
            (rolled_fwd, taps_fwd, 0, 1),
            (rolled_back, taps_back, 2, 3),
        ):
            start = rolled[eight, :]
            whole = jnp.concatenate(
                [start if k == 0 else pltpu.roll(start, 8 * k, 1) for k in range(rows // 8)],
                axis=0,
            ).astype(jnp.bfloat16)
            out[pl.ds(base, rows), :rows] = whole * masks_half[near]
            out[pl.ds(base, rows), rows:] = whole * masks_half[far]
        return carry

    lax.fori_loop(0, group_count, band, 0, unroll=2)

    lane_group = lax.div(lax.broadcasted_iota(jnp.int32, square, 1), group_size)

    def pick(parts):
        result = parts[:rows]
        for j in range(1, per_tile):
            result = jnp.where(lane_group == j, parts[j * rows : (j + 1) * rows], result)
        return result

    def spread(block):
        return jnp.concatenate(
            [
                block * jnp.where(lane_group == j, 1.0, 0.0).astype(jnp.bfloat16)
                for j in range(per_tile)
            ],
            axis=0,
        )

    def split(result):
        top, bottom = result[:slot], result[slot:]
        return jnp.where(own_first, top, bottom), jnp.where(own_first, bottom, top)

    def correlate(tile, left, right, near, far):
        product = lax.dot_general(
            spread(left), right, (((1,), (1,)), ((), ())), preferred_element_type=jnp.float32
        )
        for j in range(per_tile):
            total = None
            for k in range(rows // 8):
                here = slice(j * rows + 8 * k, j * rows + 8 * k + 8)
                mask_rows = slice(8 * k, 8 * k + 8)
                part = (
                    product[here, :rows] * masks[near, mask_rows]
                    + product[here, rows:] * masks[far, mask_rows]
                )
                if k:
                    part = pltpu.roll(part, rows - 8 * k, 1)
                total = part if total is None else total + part
            diag[pl.ds(pl.multiple_of((tile * per_tile + j) * 8, 8), 8), :] = total

    def forward(c, q, with_terms):
        tile = c * per_chunk + q
        lanes = pl.ds(pl.multiple_of(q * LANES, LANES), LANES)
        window = mixx[tile]
        lhs = taps_fwd[pl.ds(pl.multiple_of(tile * per_tile * rows, rows), per_tile * rows), :]
        hidden = pick(jnp.dot(lhs, window, preferred_element_type=jnp.float32))
        mine, theirs = split(cot[c, :, lanes].astype(jnp.float32) * hidden)
        stage_own[2, c, :, lanes] = mine.astype(jnp.bfloat16)
        stage_oth[2, c, :, lanes] = theirs.astype(jnp.bfloat16)
        if with_terms:
            correlate(tile, ggx[tile, :rows, :], window, 0, 1)

    def backward(c, q, with_terms):
        tile = c * per_chunk + q
        lanes = pl.ds(pl.multiple_of(q * LANES, LANES), LANES)
        window = ggx[tile]
        lhs = taps_back[pl.ds(pl.multiple_of(tile * per_tile * rows, rows), per_tile * rows), :]
        grad = pick(jnp.dot(lhs, window, preferred_element_type=jnp.float32))
        mine, theirs = split(grad)
        for which in range(2):
            factor = 1 - which
            stage_own[which, c, :, lanes] = (
                mine * own[factor, c, :, lanes].astype(jnp.float32)
            ).astype(jnp.bfloat16)
            stage_oth[which, c, :, lanes] = (
                theirs * rcv[factor, c, :, lanes].astype(jnp.float32)
            ).astype(jnp.bfloat16)
        if with_terms:
            correlate(tile, mixx[tile, rows:, :], window, 2, 3)

    results = (gk_hbm, gv_hbm, gq_hbm)

    def out_copy(which, c):
        return pltpu.make_async_copy(
            stage_own.at[which, c],
            results[which].at[0, 0, core, :, columns(c)],
            out_sem.at[which, c],
        )

    def back_copy(which, c):
        return pltpu.make_async_remote_copy(
            src_ref=stage_oth.at[which, c],
            dst_ref=results[which].at[0, 0, core, :, columns(c)],
            send_sem=back_send.at[which, c],
            recv_sem=back_recv.at[which, c],
            device_id=sibling,
            device_id_type=MESH,
        )

    def step(c, with_terms):
        back = chunks - 1 - c
        halo_mix(c).wait_recv()
        halo_gg(back).wait_recv()

        @pl.when(c + inflight < chunks)
        def _():
            halo_mix(c + inflight).start()
            halo_gg(back - inflight).start()

        def inner(q, carry):
            forward(c, q, with_terms)
            backward(back, q, with_terms)
            return carry

        lax.fori_loop(0, per_chunk, inner, 0)
        for which, chunk in ((2, c), (0, back), (1, back)):
            out_copy(which, chunk).start()
            back_copy(which, chunk).start()

    def step_with_terms(c, carry):
        step(c, True)
        return carry

    lax.fori_loop(0, half_chunks, step_with_terms, 0)

    reversed_half = group_count // 2
    sums = None
    for s in range(8):
        part = diag[pl.ds(s, group_count, stride=8), :]
        if s:
            part = pltpu.roll(part, rows - s, 1)
        sums = part if sums is None else sums + part
    terms[:reversed_half, :] = jnp.dot(
        sums[:reversed_half],
        flip,
        precision=lax.Precision.HIGHEST,
        preferred_element_type=jnp.float32,
    )
    terms[reversed_half:, :] = sums[reversed_half:]
    piece = group_count // team

    def piece_rows(index):
        return pl.ds(pl.multiple_of(index * piece, piece), piece)

    def remote(src, dst, send, recv, device):
        return pltpu.make_async_remote_copy(
            src_ref=src,
            dst_ref=dst,
            send_sem=send,
            recv_sem=recv,
            device_id=device,
            device_id_type=MESH,
        )

    def exchange(ring, count, here, buffer, source, send, recv):
        copies = []
        for k in range(1, count):
            index, device = ring(k)
            copy = remote(
                source(index), buffer.at[here], send.at[k - 1], recv.at[k - 1], device
            )
            copy.start()
            copies.append(copy)
        return copies

    def arrive(ring, count, buffer, send, recv):
        for k in range(1, count):
            index, device = ring(count - k)
            remote(
                buffer.at[index], buffer.at[index], send.at[k - 1], recv.at[k - 1], device
            ).wait_recv()

    def total_of(buffer, count):
        total = buffer[0]
        for k in range(1, count):
            total = total + buffer[k]
        return total

    sent = []
    piece_one[place] = terms[piece_rows(place), :]
    sent += exchange(
        member, team, place, piece_one, lambda i: terms.at[piece_rows(i)], one_send, one_recv
    )

    stages = [0, 1, 2, 3]

    def advance(stage):
        if stage == 0:
            arrive(member, team, piece_one, one_send, one_recv)
            piece_two[y] = total_of(piece_one, team)
            return exchange(
                along_y, y_count, y, piece_two, lambda i: piece_two.at[y], two_send, two_recv
            )
        if stage == 1:
            arrive(along_y, y_count, piece_two, two_send, two_recv)
            piece_three[z] = total_of(piece_two, y_count)
            return exchange(
                along_z, z_count, z, piece_three, lambda i: piece_three.at[z], three_send, three_recv
            )
        if stage == 2:
            arrive(along_z, z_count, piece_three, three_send, three_recv)
            diag[piece_rows(place), :] = total_of(piece_three, z_count) * scale
            copies = []
            for k in range(1, team):
                index, device = member(k)
                copy = remote(
                    diag.at[piece_rows(place)],
                    diag.at[piece_rows(place)],
                    four_send.at[k - 1],
                    four_recv.at[k - 1],
                    device,
                )
                copy.start()
                copies.append(copy)
            return copies
        for k in range(1, team):
            index, device = member(team - k)
            remote(
                diag.at[piece_rows(index)],
                diag.at[piece_rows(index)],
                four_send.at[k - 1],
                four_recv.at[k - 1],
                device,
            ).wait_recv()
        return []

    for c in range(half_chunks, chunks):
        step(c, False)
        if stages:
            sent += advance(stages.pop(0))
    while stages:
        sent += advance(stages.pop(0))
    final = pltpu.make_async_copy(diag.at[pl.ds(0, group_count)], gf_hbm, final_sem)
    final.start()

    for copy in sent:
        copy.wait_send()

    def finish(c, carry):
        halo_mix(c).wait_send()
        halo_gg(c).wait_send()
        for which in range(3):
            swap_copy(which, c).wait_send()
            out_copy(which, c).wait()
            back_copy(which, c).wait()
        return carry

    lax.fori_loop(0, chunks, finish, 0)
    final.wait()


def body(dims, chunks, inflight, *operands):
    query_tiles, cotangent, filters = operands[0], operands[3], operands[4]
    slot, features = query_tiles.shape[3:]
    rows = cotangent.shape[1]
    groups = filters.shape[0]
    z_count, y_count, x_count = dims
    team = 2 * x_count
    piece = groups // team
    width = features // chunks
    tiles = features // LANES
    half, single = jnp.bfloat16, jnp.float32
    total = 2 * rows * z_count * y_count * x_count * (features // groups)
    anywhere = pl.BlockSpec(memory_space=pl.ANY)
    dma = pltpu.SemaphoreType.DMA
    return pl.pallas_call(
        functools.partial(kernel_body, dims, chunks, inflight, 1.0 / math.sqrt(total)),
        out_shape=(
            jax.ShapeDtypeStruct(query_tiles.shape, half),
            jax.ShapeDtypeStruct(query_tiles.shape, half),
            jax.ShapeDtypeStruct(query_tiles.shape, half),
            jax.ShapeDtypeStruct(filters.shape, single),
        ),
        in_specs=[anywhere] * 4
        + [
            pl.BlockSpec(memory_space=pltpu.VMEM),
            pl.BlockSpec(memory_space=pltpu.SMEM),
            pl.BlockSpec(memory_space=pltpu.SMEM),
        ],
        out_specs=[anywhere] * 4,
        scratch_shapes=[
            pltpu.VMEM((3, chunks, slot, width), half),
            pltpu.VMEM((3, chunks, slot, width), half),
            pltpu.VMEM((chunks, rows, width), half),
            pltpu.VMEM((tiles, 2 * rows, LANES), half),
            pltpu.VMEM((tiles, 2 * rows, LANES), half),
            pltpu.VMEM((groups * rows, 2 * rows), half),
            pltpu.VMEM((groups * rows, 2 * rows), half),
            pltpu.VMEM((groups * 8, rows), single),
            pltpu.VMEM((groups * 8, rows), single),
            pltpu.VMEM((4, rows, rows), half),
            pltpu.VMEM((4, rows, rows), single),
            pltpu.VMEM((groups * 8, rows), single),
            pltpu.VMEM((groups, rows), single),
            pltpu.VMEM((3, chunks, slot, width), half),
            pltpu.VMEM((3, chunks, slot, width), half),
            pltpu.VMEM((team, piece, rows), single),
            pltpu.VMEM((y_count, piece, rows), single),
            pltpu.VMEM((z_count, piece, rows), single),
            dma((3, chunks)),
            dma((chunks,)),
            dma((3, chunks)),
            dma((3, chunks)),
            dma((chunks,)),
            dma((chunks,)),
            dma((chunks,)),
            dma((chunks,)),
            dma((3, chunks)),
            dma((3, chunks)),
            dma((3, chunks)),
            dma((team - 1,)),
            dma((team - 1,)),
            dma((y_count - 1,)),
            dma((y_count - 1,)),
            dma((z_count - 1,)),
            dma((z_count - 1,)),
            dma((team - 1,)),
            dma((team - 1,)),
            dma,
        ],
        compiler_params=pltpu.CompilerParams(
            collective_id=0, has_side_effects=True, vmem_limit_bytes=48 * 1024 * 1024
        ),
        cost_estimate=pl.CostEstimate(
            flops=12 * rows * rows * features, bytes_accessed=14 * rows * features, transcendentals=0
        ),
    )(*operands)


def build(mesh, dims, chunks, inflight):
    placed = (
        P("dp", "seq", None, None, None),
        P("dp", "seq", None, None, None),
        P("dp", "seq", None, None, None),
        P("dp", "seq", None),
        P(),
        P(),
        P(None, "seq", None),
    )
    return jax.shard_map(
        functools.partial(body, dims, chunks, inflight),
        mesh=mesh,
        in_specs=placed,
        out_specs=(
            P("dp", "seq", None, None, None),
            P("dp", "seq", None, None, None),
            P("dp", "seq", None, None, None),
            P(),
        ),
        check_vma=False,
    )


def solution(mesh):
    return build(mesh, (8, 4, 4), 8, 8)
```

time: 532 us -> 61.9 us (0.12); the launches traced: 523 us -> 61.6 us
  local copies, waits for them, and re-layouts: 233 us -> 8.1 us
  waiting for transfers between devices: 106 us -> 0 us
  matrix products: 80.3 us -> 0 us
  other arithmetic: 56.3 us -> 0 us
  Pallas kernels: 0 us -> 52.9 us
  starting transfers between devices: 19.2 us -> 0 us
  between operations: 15.3 us -> 0.66 us
  blocking collectives: 13.4 us -> 0 us
    psum x1 -> x0, waiting for transfers between devices: 104 us -> none  [body(): total_terms = lax.psum(filter_terms, ('dp', 'seq'))]
    dot_general x30 -> x0, matrix products: 80.3 us -> none  [the longest x8 28.6 us: forward_block(): jnp.einsum('tgc,egc->gte', gradient, features, preferred_element_type=jnp...]
    mul x24 -> x0, local copies, waits for them, and re-layouts: 61.6 us -> none  [the longest x8 22.2 us: forward_block(): jnp.einsum('tgc,egc->gte', gradient, features, preferred_element_type=jnp...]
    reshape x34 -> x0, local copies, waits for them, and re-layouts: 57.4 us -> none  [the longest x8 19.3 us: forward_block(): skewed = jnp.pad(correl.reshape(group_count, block_rows * span), ((0, 0),...]
    slice x20 -> x0, local copies, waits for them, and re-layouts: 54 us -> none  [the longest x8 29.1 us: forward_block(): window = extended[start_row:start_row + span]]
    pallas_call x0 -> x1, Pallas kernels: none -> 52.9 us  [body(): pl.pallas_call(functools.partial(kernel_body, dims, chunks, inflight, 1.0...]
    pad x8 -> x0, local copies, waits for them, and re-layouts: 19.1 us -> none  [forward_block(): jnp.pad(correl.reshape(group_count, block_rows * span), ((0, 0), (0, bloc...]
    all_to_all x3 -> x0, starting transfers between devices: 15.5 us -> none  [the longest x1 6.82 us: body(): lax.all_to_all(value_home, 'dp', split_axis=0, concat_axis=0, tiled=True)]
  transfers between devices with their start and end apart: 6 -> 0, of which waited for: 2 -> 0; matrix products, arithmetic and copies ran while one was open for 68% -> 0% of each run, Pallas kernels for 0% -> 0%
where the time goes in v1:
time: 61.9 us; the launch traced here: 61.6 us
  Pallas kernels  52.9 us (85%)
  local copies, waits for them, and re-layouts  8.1 us (13%)
  between operations  0.66 us (1%)
    pallas_call x1, Pallas kernels, body(): pl.pallas_call(functools.partial(kernel_body, dims, chunks, inflight, 1.0...  52.9 us
    unnamed x14, local copies, waits for them, and re-layouts  8.1 us

profile of v1, /device:TPU:1, one launch (start us, length us, event | category | flops | bytes accessed | tf_op | source)
XLA Modules:
  0.0 61.6 jit_solution(15276593667778438617)
XLA Ops:
  0.6 0.0 copy-start
  0.6 1.2 %copy-done = bf16[1,1,2,64,4096]{4,3,2,1,0:T(8,128)(2,1)S(1)} copy-done((bf16[1,1,2,64,4096]{4,3,2,1,0:T(8,128)(2,1)S(1)}, bf16[1,1,2,64,4096]{4,3,2,1,0:T(8,128)(2,1)}, u32[]{:S(2)}) %copy-start) | copy-done | bytes 1048600
  1.9 0.0 copy-start.1
  1.9 1.2 %copy-done.1 = bf16[1,1,2,64,4096]{4,3,2,1,0:T(8,128)(2,1)S(1)} copy-done((bf16[1,1,2,64,4096]{4,3,2,1,0:T(8,128)(2,1)S(1)}, bf16[1,1,2,64,4096]{4,3,2,1,0:T(8,128)(2,1)}, u32[]{:S(2)}) %copy-start.1) | copy-done | bytes 1048600
  3.1 0.0 copy-start.2
  3.1 0.8 %copy-done.2 = bf16[128,128]{1,0:T(8,128)(2,1)S(1)} copy-done((bf16[128,128]{1,0:T(8,128)(2,1)S(1)}, bf16[128,128]{1,0:T(8,128)(2,1)}, u32[]{:S(2)}) %copy-start.2) | copy-done | bytes 32792
  3.8 0.0 copy-start.3
  3.8 0.7 %copy-done.3 = s32[2,8]{1,0:T(2,128)S(1)} copy-done((s32[2,8]{1,0:T(2,128)S(1)}, s32[2,8]{1,0:T(2,128)}, u32[]{:S(2)}) %copy-start.3) | copy-done | bytes 88
  4.5 0.0 copy-start.4
  4.5 0.7 %copy-done.4 = s32[2,1,2]{2,1,0:T(1,128)S(1)} copy-done((s32[2,1,2]{2,1,0:T(1,128)S(1)}, s32[2,1,2]{2,1,0:T(1,128)}, u32[]{:S(2)}) %copy-start.4) | copy-done | bytes 40
  5.2 52.9 %shard_map.102 = (bf16[1,1,2,64,4096]{4,3,2,1,0:T(8,128)(2,1)S(1)}, bf16[1,1,2,64,4096]{4,3,2,1,0:T(8,128)(2,1)S(1)}, bf16[1,1,2,64,4096]{4,3,2,1,0:T(8,128)(2,1)S(1)}, f32[128,128]{1,0:T(8,128)S(1)}) custom-call(bf16[1,1,2,64,4096]{4,3,2,1,0:T(8,128)(2,1)S(1)} %copy-done, bf16[1,1,2,64,4096]{4,3,2,1,0:T(8,128)(2,1)S(1)} %copy-done.1, ...), custom_call_target="tpu_custom_call" | custom-call | flops 805306368 | bytes 7340032 | tf_op jit(solution)/shard_map/pallas_call | solution.py:531
  58.1 1.0 %copy.15 = bf16[1,1,2,64,4096]{4,3,2,1,0:T(8,128)(2,1)} copy(bf16[1,1,2,64,4096]{4,3,2,1,0:T(8,128)(2,1)S(1)} %get-tuple-element.8) | data formatting | bytes 2097152
  59.1 1.0 %copy.16 = bf16[1,1,2,64,4096]{4,3,2,1,0:T(8,128)(2,1)} copy(bf16[1,1,2,64,4096]{4,3,2,1,0:T(8,128)(2,1)S(1)} %get-tuple-element.9) | data formatting | bytes 2097152
  60.0 1.0 %copy.17 = bf16[1,1,2,64,4096]{4,3,2,1,0:T(8,128)(2,1)} copy(bf16[1,1,2,64,4096]{4,3,2,1,0:T(8,128)(2,1)S(1)} %get-tuple-element.10) | data formatting | bytes 2097152
  61.0 0.6 %copy.18 = f32[128,128]{1,0:T(8,128)} copy(f32[128,128]{1,0:T(8,128)S(1)} %get-tuple-element.11) | data formatting | bytes 131072
Async XLA Ops:
  0.6 1.2 %copy-start = (bf16[1,1,2,64,4096]{4,3,2,1,0:T(8,128)(2,1)S(1)}, bf16[1,1,2,64,4096]{4,3,2,1,0:T(8,128)(2,1)}, u32[]{:S(2)}) copy-start(bf16[1,1,2,64,4096]{4,3,2,1,0:T(8,128)(2,1)} %query_hbm.1) | copy-start | bytes 3145732
  1.9 1.2 %copy-start.1 = (bf16[1,1,2,64,4096]{4,3,2,1,0:T(8,128)(2,1)S(1)}, bf16[1,1,2,64,4096]{4,3,2,1,0:T(8,128)(2,1)}, u32[]{:S(2)}) copy-start(bf16[1,1,2,64,4096]{4,3,2,1,0:T(8,128)(2,1)} %key_hbm.1) | copy-start | bytes 3145732
  3.1 0.8 %copy-start.2 = (bf16[128,128]{1,0:T(8,128)(2,1)S(1)}, bf16[128,128]{1,0:T(8,128)(2,1)}, u32[]{:S(2)}) copy-start(bf16[128,128]{1,0:T(8,128)(2,1)} %filters_ref.1) | copy-start | bytes 98308
  3.8 0.7 %copy-start.3 = (s32[2,8]{1,0:T(2,128)S(1)}, s32[2,8]{1,0:T(2,128)}, u32[]{:S(2)}) copy-start(s32[2,8]{1,0:T(2,128)} %doc_ref.1) | copy-start | bytes 196
  4.5 0.7 %copy-start.4 = (s32[2,1,2]{2,1,0:T(1,128)S(1)}, s32[2,1,2]{2,1,0:T(1,128)}, u32[]{:S(2)}) copy-start(s32[2,1,2]{2,1,0:T(1,128)} %arrival_ref.1) | copy-start | bytes 52

commit v2 on v1

--- a/solution.py
+++ b/solution.py
@@ -10,24 +10,27 @@
 
 MESH = pl.DeviceIdType.MESH
 LANES = 128
+VMEM_BYTES = 60 * 1024 * 1024
 
 
 def kernel_body(
     dims,
     chunks,
-    inflight,
     scale,
     query_hbm,
     key_hbm,
     value_hbm,
     cot_hbm,
-    filters_ref,
-    doc_ref,
-    arrival_ref,
+    filters_hbm,
+    doc_hbm,
+    arrival_hbm,
     gq_hbm,
     gk_hbm,
     gv_hbm,
     gf_hbm,
+    filters_ref,
+    doc_ref,
+    arrival_ref,
     own,
     rcv,
     cot,
@@ -46,8 +49,8 @@
     piece_one,
     piece_two,
     piece_three,
+    small_sem,
     own_sem,
-    cot_sem,
     swap_send,
     swap_recv,
     mix_send,
@@ -71,8 +74,8 @@
     seq_count = z_count * y_count * x_count
     group_count, kernel = filters_ref.shape
     rows = kernel
-    slot = own.shape[2]
-    width = own.shape[3]
+    slot = rcv.shape[2]
+    width = rcv.shape[3]
     tile_count = mixx.shape[0]
     per_chunk = tile_count // chunks
     per_tile = group_count // tile_count
@@ -105,20 +108,34 @@
     def columns(c):
         return pl.ds(pl.multiple_of(c * width, width), width)
 
+    barrier = pltpu.get_barrier_semaphore()
+    partners = [sibling, following, previous]
+    partners += [member(k)[1] for k in range(1, team)]
+    partners += [along_y(k)[1] for k in range(1, y_count)]
+    partners += [along_z(k)[1] for k in range(1, z_count)]
+    for partner in partners:
+        pl.semaphore_signal(barrier, inc=1, device_id=partner, device_id_type=MESH)
+
+    small = [
+        pltpu.make_async_copy(doc_hbm, doc_ref, small_sem.at[0]),
+        pltpu.make_async_copy(filters_hbm, filters_ref, small_sem.at[1]),
+        pltpu.make_async_copy(arrival_hbm, arrival_ref, small_sem.at[2]),
+    ]
+    for copy in small:
+        copy.start()
+
     sources = (key_hbm, value_hbm, query_hbm)
 
     def chunk_of(which, c):
         return chunks - 1 - c if which == 2 else c
 
-    def own_copy(which, c):
-        return pltpu.make_async_copy(
-            sources[which].at[0, 0, core, :, columns(c)],
-            own.at[which, c],
-            own_sem.at[which, c],
-        )
-
-    def cot_copy(c):
-        return pltpu.make_async_copy(cot_hbm.at[0, :, columns(c)], cot.at[c], cot_sem.at[c])
+    own_copies = [
+        pltpu.make_async_copy(sources[which].at[0, 0, core], own.at[which], own_sem.at[which])
+        for which in range(3)
+    ]
+    own_copies.append(pltpu.make_async_copy(cot_hbm.at[0], cot, own_sem.at[3]))
+    for copy in own_copies:
+        copy.start()
 
     def swap_copy(which, c):
         return pltpu.make_async_remote_copy(
@@ -130,18 +147,17 @@
             device_id_type=MESH,
         )
 
-    for c in range(chunks):
+    pl.semaphore_wait(barrier, len(partners))
+
+    def swap(c):
         for which in range(3):
-            own_copy(which, chunk_of(which, c)).start()
-        cot_copy(chunks - 1 - c).start()
-
-    barrier = pltpu.get_barrier_semaphore()
-    partners = [sibling, following, previous]
-    partners += [member(k)[1] for k in range(1, team)]
-    partners += [along_y(k)[1] for k in range(1, y_count)]
-    partners += [along_z(k)[1] for k in range(1, z_count)]
-    for partner in partners:
-        pl.semaphore_signal(barrier, inc=1, device_id=partner, device_id_type=MESH)
+            swap_copy(which, chunk_of(which, c)).start()
+
+    ahead = 2
+    for c in range(ahead):
+        swap(c)
+    for copy in small:
+        copy.wait()
 
     square = (rows, rows)
     row = lax.broadcasted_iota(jnp.int32, square, 0)
@@ -175,11 +191,6 @@
 
     flip = as_mask(lax.rem(row + col, kernel) == 0)
 
-    pl.semaphore_wait(barrier, len(partners))
-    for c in range(chunks):
-        for which in range(3):
-            swap_copy(which, chunk_of(which, c)).start()
-
     straight = filters_ref[...].astype(jnp.float32)
     turned = jnp.dot(
         filters_ref[...], flip.astype(jnp.bfloat16), preferred_element_type=jnp.float32
@@ -187,6 +198,9 @@
     for s in range(8):
         rolled_fwd[pl.ds(s, group_count, stride=8), :] = pltpu.roll(turned, s, 1)
         rolled_back[pl.ds(s, group_count, stride=8), :] = pltpu.roll(straight, s, 1)
+
+    for copy in own_copies:
+        copy.wait()
 
     held = arrival_ref[core, 0, core]
     own_first = jnp.full((slot, LANES), held, jnp.int32) == 0
@@ -218,37 +232,49 @@
             device_id_type=MESH,
         )
 
+    def halos(c):
+        halo_mix(c).start()
+        halo_gg(chunks - 1 - c).start()
+
+    def lanes_of(c, q):
+        return pl.ds(pl.multiple_of(c * width + q * LANES, LANES), LANES)
+
+    early = 3 * chunks // 4
+
     def assemble(c, carry):
         back = chunks - 1 - c
+
+        @pl.when(c + ahead < chunks)
+        def _():
+            swap(c + ahead)
+
         for which in range(2):
-            own_copy(which, c).wait()
             swap_copy(which, c).wait_recv()
         for q in range(per_chunk):
             lanes = slice(q * LANES, (q + 1) * LANES)
-            mine = own[0, c, :, lanes].astype(jnp.float32) * own[1, c, :, lanes].astype(jnp.float32)
+            here = lanes_of(c, q)
+            mine = own[0, :, here].astype(jnp.float32) * own[1, :, here].astype(jnp.float32)
             received = rcv[0, c, :, lanes].astype(jnp.float32) * rcv[1, c, :, lanes].astype(
                 jnp.float32
             )
             mixx[c * per_chunk + q, rows:, :] = in_order(mine, received).astype(jnp.bfloat16)
 
-        @pl.when(c < inflight)
+        @pl.when(c < early)
         def _():
             halo_mix(c).start()
 
-        own_copy(2, back).wait()
         swap_copy(2, back).wait_recv()
-        cot_copy(back).wait()
         for q in range(per_chunk):
             lanes = slice(q * LANES, (q + 1) * LANES)
+            here = lanes_of(back, q)
             gate = in_order(
-                own[2, back, :, lanes].astype(jnp.float32),
-                rcv[2, back, :, lanes].astype(jnp.float32),
+                own[2, :, here].astype(jnp.float32), rcv[2, back, :, lanes].astype(jnp.float32)
             )
             ggx[back * per_chunk + q, :rows, :] = (
-                gate * cot[back, :, lanes].astype(jnp.float32)
+                gate * cot[:, here].astype(jnp.float32)
             ).astype(jnp.bfloat16)
 
-        @pl.when(c < inflight)
+        @pl.when(c < early)
         def _():
             halo_gg(back).start()
 
@@ -272,7 +298,7 @@
             out[pl.ds(base, rows), rows:] = whole * masks_half[far]
         return carry
 
-    lax.fori_loop(0, group_count, band, 0, unroll=2)
+    lax.fori_loop(0, group_count, band, 0, unroll=8)
 
     lane_group = lax.div(lax.broadcasted_iota(jnp.int32, square, 1), group_size)
 
@@ -313,35 +339,29 @@
                 total = part if total is None else total + part
             diag[pl.ds(pl.multiple_of((tile * per_tile + j) * 8, 8), 8), :] = total
 
-    def forward(c, q, with_terms):
+    def forward(c, q):
         tile = c * per_chunk + q
         lanes = pl.ds(pl.multiple_of(q * LANES, LANES), LANES)
-        window = mixx[tile]
         lhs = taps_fwd[pl.ds(pl.multiple_of(tile * per_tile * rows, rows), per_tile * rows), :]
-        hidden = pick(jnp.dot(lhs, window, preferred_element_type=jnp.float32))
-        mine, theirs = split(cot[c, :, lanes].astype(jnp.float32) * hidden)
+        hidden = pick(jnp.dot(lhs, mixx[tile], preferred_element_type=jnp.float32))
+        mine, theirs = split(cot[:, lanes_of(c, q)].astype(jnp.float32) * hidden)
         stage_own[2, c, :, lanes] = mine.astype(jnp.bfloat16)
         stage_oth[2, c, :, lanes] = theirs.astype(jnp.bfloat16)
-        if with_terms:
-            correlate(tile, ggx[tile, :rows, :], window, 0, 1)
-
-    def backward(c, q, with_terms):
+
+    def backward(c, q):
         tile = c * per_chunk + q
         lanes = pl.ds(pl.multiple_of(q * LANES, LANES), LANES)
-        window = ggx[tile]
         lhs = taps_back[pl.ds(pl.multiple_of(tile * per_tile * rows, rows), per_tile * rows), :]
-        grad = pick(jnp.dot(lhs, window, preferred_element_type=jnp.float32))
+        grad = pick(jnp.dot(lhs, ggx[tile], preferred_element_type=jnp.float32))
         mine, theirs = split(grad)
         for which in range(2):
             factor = 1 - which
             stage_own[which, c, :, lanes] = (
-                mine * own[factor, c, :, lanes].astype(jnp.float32)
+                mine * own[factor, :, lanes_of(c, q)].astype(jnp.float32)
             ).astype(jnp.bfloat16)
             stage_oth[which, c, :, lanes] = (
                 theirs * rcv[factor, c, :, lanes].astype(jnp.float32)
             ).astype(jnp.bfloat16)
-        if with_terms:
-            correlate(tile, mixx[tile, rows:, :], window, 2, 3)
 
     results = (gk_hbm, gv_hbm, gq_hbm)
 
@@ -362,31 +382,46 @@
             device_id_type=MESH,
         )
 
-    def step(c, with_terms):
+    def arrived(c):
+        halo_mix(c).wait_recv()
+        halo_gg(chunks - 1 - c).wait_recv()
+
+    def terms_step(c, carry):
         back = chunks - 1 - c
-        halo_mix(c).wait_recv()
-        halo_gg(back).wait_recv()
-
-        @pl.when(c + inflight < chunks)
+        arrived(c)
+
+        def inner(q, inner_carry):
+            tile = c * per_chunk + q
+            correlate(tile, ggx[tile, :rows, :], mixx[tile], 0, 1)
+            tile = back * per_chunk + q
+            correlate(tile, mixx[tile, rows:, :], ggx[tile], 2, 3)
+            return inner_carry
+
+        lax.fori_loop(0, per_chunk, inner, 0, unroll=True)
+        return carry
+
+    def step(c, carry):
+        back = chunks - 1 - c
+
+        @pl.when(c >= half_chunks)
         def _():
-            halo_mix(c + inflight).start()
-            halo_gg(back - inflight).start()
-
-        def inner(q, carry):
-            forward(c, q, with_terms)
-            backward(back, q, with_terms)
-            return carry
-
-        lax.fori_loop(0, per_chunk, inner, 0)
+            arrived(c)
+
+        def inner(q, inner_carry):
+            forward(c, q)
+            backward(back, q)
+            return inner_carry
+
+        lax.fori_loop(0, per_chunk, inner, 0, unroll=True)
         for which, chunk in ((2, c), (0, back), (1, back)):
             out_copy(which, chunk).start()
             back_copy(which, chunk).start()
-
-    def step_with_terms(c, carry):
-        step(c, True)
         return carry
 
-    lax.fori_loop(0, half_chunks, step_with_terms, 0)
+    before = chunks // 4
+    lax.fori_loop(0, half_chunks - 1, terms_step, 0)
+    lax.fori_loop(0, before, step, 0)
+    terms_step(half_chunks - 1, 0)
 
     reversed_half = group_count // 2
     sums = None
@@ -441,36 +476,44 @@
             total = total + buffer[k]
         return total
 
+    own_piece = pltpu.make_async_copy(
+        diag.at[piece_rows(place)], gf_hbm.at[piece_rows(place)], final_sem
+    )
     sent = []
     piece_one[place] = terms[piece_rows(place), :]
     sent += exchange(
         member, team, place, piece_one, lambda i: terms.at[piece_rows(i)], one_send, one_recv
     )
 
-    stages = [0, 1, 2, 3]
+    middle = (
+        (along_z, z_count, z, piece_three, three_send, three_recv),
+        (along_y, y_count, y, piece_two, two_send, two_recv),
+    )
 
     def advance(stage):
         if stage == 0:
             arrive(member, team, piece_one, one_send, one_recv)
-            piece_two[y] = total_of(piece_one, team)
-            return exchange(
-                along_y, y_count, y, piece_two, lambda i: piece_two.at[y], two_send, two_recv
-            )
+            ring, count, here, buffer, send, recv = middle[0]
+            buffer[here] = total_of(piece_one, team)
+            return exchange(ring, count, here, buffer, lambda i: buffer.at[here], send, recv)
         if stage == 1:
-            arrive(along_y, y_count, piece_two, two_send, two_recv)
-            piece_three[z] = total_of(piece_two, y_count)
-            return exchange(
-                along_z, z_count, z, piece_three, lambda i: piece_three.at[z], three_send, three_recv
-            )
+            ring, count, here, buffer, send, recv = middle[0]
+            arrive(ring, count, buffer, send, recv)
+            total = total_of(buffer, count)
+            ring, count, here, buffer, send, recv = middle[1]
+            buffer[here] = total
+            return exchange(ring, count, here, buffer, lambda i: buffer.at[here], send, recv)
         if stage == 2:
-            arrive(along_z, z_count, piece_three, three_send, three_recv)
-            diag[piece_rows(place), :] = total_of(piece_three, z_count) * scale
+            ring, count, here, buffer, send, recv = middle[1]
+            arrive(ring, count, buffer, send, recv)
+            diag[piece_rows(place), :] = total_of(buffer, count) * scale
+            own_piece.start()
             copies = []
             for k in range(1, team):
                 index, device = member(k)
                 copy = remote(
                     diag.at[piece_rows(place)],
-                    diag.at[piece_rows(place)],
+                    gf_hbm.at[piece_rows(place)],
                     four_send.at[k - 1],
                     four_recv.at[k - 1],
                     device,
@@ -481,22 +524,23 @@
         for k in range(1, team):
             index, device = member(team - k)
             remote(
-                diag.at[piece_rows(index)],
-                diag.at[piece_rows(index)],
+                gf_hbm.at[piece_rows(index)],
+                gf_hbm.at[piece_rows(index)],
                 four_send.at[k - 1],
                 four_recv.at[k - 1],
                 device,
             ).wait_recv()
         return []
 
-    for c in range(half_chunks, chunks):
-        step(c, False)
-        if stages:
-            sent += advance(stages.pop(0))
-    while stages:
-        sent += advance(stages.pop(0))
-    final = pltpu.make_async_copy(diag.at[pl.ds(0, group_count)], gf_hbm, final_sem)
-    final.start()
+    middle_chunk = (early + chunks) // 2
+    late = [early, middle_chunk, middle_chunk, chunks]
+    ends = [before, chunks // 2, 5 * chunks // 8, 7 * chunks // 8, chunks]
+    for stage in range(4):
+        if stage < 3:
+            for c in range(late[stage], late[stage + 1]):
+                halos(c)
+        lax.fori_loop(ends[stage], ends[stage + 1], step, 0)
+        sent += advance(stage)
 
     for copy in sent:
         copy.wait_send()
@@ -511,10 +555,29 @@
         return carry
 
     lax.fori_loop(0, chunks, finish, 0)
-    final.wait()
-
-
-def body(dims, chunks, inflight, *operands):
+    own_piece.wait()
+
+
+def hand_over(count, *refs):
+    copies = []
+    for i in range(count):
+        source, target, sems = refs[i], refs[count + i], refs[-1]
+        if len(source.shape) == 2:
+            copies.append(pltpu.make_async_copy(source, target, sems.at[2 * i]))
+            continue
+        for j in range(2):
+            copies.append(
+                pltpu.make_async_copy(
+                    source.at[0, 0, j], target.at[0, 0, j], sems.at[2 * i + j]
+                )
+            )
+    for copy in copies:
+        copy.start()
+    for copy in copies:
+        copy.wait()
+
+
+def body(dims, chunks, *operands):
     query_tiles, cotangent, filters = operands[0], operands[3], operands[4]
     slot, features = query_tiles.shape[3:]
     rows = cotangent.shape[1]
@@ -528,25 +591,23 @@
     total = 2 * rows * z_count * y_count * x_count * (features // groups)
     anywhere = pl.BlockSpec(memory_space=pl.ANY)
     dma = pltpu.SemaphoreType.DMA
-    return pl.pallas_call(
-        functools.partial(kernel_body, dims, chunks, inflight, 1.0 / math.sqrt(total)),
+    results = pl.pallas_call(
+        functools.partial(kernel_body, dims, chunks, 1.0 / math.sqrt(total)),
         out_shape=(
-            jax.ShapeDtypeStruct(query_tiles.shape, half),
-            jax.ShapeDtypeStruct(query_tiles.shape, half),
-            jax.ShapeDtypeStruct(query_tiles.shape, half),
-            jax.ShapeDtypeStruct(filters.shape, single),
+            pltpu.VMEM(query_tiles.shape, half),
+            pltpu.VMEM(query_tiles.shape, half),
+            pltpu.VMEM(query_tiles.shape, half),
+            pltpu.VMEM(filters.shape, single),
         ),
-        in_specs=[anywhere] * 4
-        + [
-            pl.BlockSpec(memory_space=pltpu.VMEM),
-            pl.BlockSpec(memory_space=pltpu.SMEM),
-            pl.BlockSpec(memory_space=pltpu.SMEM),
-        ],
+        in_specs=[anywhere] * 7,
         out_specs=[anywhere] * 4,
         scratch_shapes=[
+            pltpu.VMEM(filters.shape, half),
+            pltpu.SMEM(operands[5].shape, jnp.int32),
+            pltpu.SMEM(operands[6].shape, jnp.int32),
+            pltpu.VMEM((3, slot, features), half),
             pltpu.VMEM((3, chunks, slot, width), half),
-            pltpu.VMEM((3, chunks, slot, width), half),
-            pltpu.VMEM((chunks, rows, width), half),
+            pltpu.VMEM((rows, features), half),
             pltpu.VMEM((tiles, 2 * rows, LANES), half),
             pltpu.VMEM((tiles, 2 * rows, LANES), half),
             pltpu.VMEM((groups * rows, 2 * rows), half),
@@ -562,8 +623,8 @@
             pltpu.VMEM((team, piece, rows), single),
             pltpu.VMEM((y_count, piece, rows), single),
             pltpu.VMEM((z_count, piece, rows), single),
-            dma((3, chunks)),
-            dma((chunks,)),
+            dma((3,)),
+            dma((4,)),
             dma((3, chunks)),
             dma((3, chunks)),
             dma((chunks,)),
@@ -584,15 +645,24 @@
             dma,
         ],
         compiler_params=pltpu.CompilerParams(
-            collective_id=0, has_side_effects=True, vmem_limit_bytes=48 * 1024 * 1024
+            collective_id=0, has_side_effects=True, vmem_limit_bytes=VMEM_BYTES
         ),
         cost_estimate=pl.CostEstimate(
             flops=12 * rows * rows * features, bytes_accessed=14 * rows * features, transcendentals=0
         ),
     )(*operands)
-
-
-def build(mesh, dims, chunks, inflight):
+    count = len(results)
+    return pl.pallas_call(
+        functools.partial(hand_over, count),
+        out_shape=tuple(jax.ShapeDtypeStruct(r.shape, r.dtype) for r in results),
+        in_specs=[anywhere] * count,
+        out_specs=[anywhere] * count,
+        scratch_shapes=[dma((2 * count,))],
+        compiler_params=pltpu.CompilerParams(vmem_limit_bytes=2 * 1024 * 1024),
+    )(*results)
+
+
+def build(mesh, dims, chunks):
     placed = (
         P("dp", "seq", None, None, None),
         P("dp", "seq", None, None, None),
@@ -603,7 +673,7 @@
         P(None, "seq", None),
     )
     return jax.shard_map(
-        functools.partial(body, dims, chunks, inflight),
+        functools.partial(body, dims, chunks),
         mesh=mesh,
         in_specs=placed,
         out_specs=(
@@ -617,4 +687,4 @@
 
 
 def solution(mesh):
-    return build(mesh, (8, 4, 4), 8, 8)
+    return build(mesh, (8, 4, 4), 8)

time: 61.9 us -> 51.3 us (0.83)
  local copies, waits for them, and re-layouts: 8.1 us -> 0 us
  Pallas kernels: 52.9 us -> 50.6 us
    unnamed x14 -> x0, local copies, waits for them, and re-layouts: 8.1 us -> none
    pallas_call x1 -> x2, Pallas kernels: 52.9 us -> 50.6 us  [the longest x1 48.9 us: body(): pl.pallas_call(functools.partial(kernel_body, dims, chunks, 1.0 / math.sq...]
where the time goes in v2:
time: 51.3 us
  Pallas kernels  50.6 us (99%)
  between operations  0.64 us (1%)
    pallas_call x1, Pallas kernels, body(): pl.pallas_call(functools.partial(kernel_body, dims, chunks, 1.0 / math.sq...  48.9 us
    pallas_call x1, Pallas kernels, body(): pl.pallas_call(functools.partial(hand_over, count), out_shape=tuple((jax....  1.74 us

profile of v2, /device:TPU:1, one launch (start us, length us, event | category | flops | bytes accessed | tf_op | source)
XLA Modules:
  0.0 51.3 jit_solution(15287167782898934748)
XLA Ops:
  0.6 48.9 %shard_map.102 = (bf16[1,1,2,64,4096]{4,3,2,1,0:T(8,128)(2,1)S(1)}, bf16[1,1,2,64,4096]{4,3,2,1,0:T(8,128)(2,1)S(1)}, bf16[1,1,2,64,4096]{4,3,2,1,0:T(8,128)(2,1)S(1)}, f32[128,128]{1,0:T(8,128)S(1)}) custom-call(bf16[1,1,2,64,4096]{4,3,2,1,0:T(8,128)(2,1)} %query_hbm.1, bf16[1,1,2,64,4096]{4,3,2,1,0:T(8,128)(2,1)} %key_hbm.1, ...), custom_call_target="tpu_custom_call" | custom-call | flops 805306368 | bytes 7340032 | tf_op jit(solution)/shard_map/pallas_call | solution.py:594
  49.5 1.7 %shard_map.103 = (bf16[1,1,2,64,4096]{4,3,2,1,0:T(8,128)(2,1)}, bf16[1,1,2,64,4096]{4,3,2,1,0:T(8,128)(2,1)}, bf16[1,1,2,64,4096]{4,3,2,1,0:T(8,128)(2,1)}, f32[128,128]{1,0:T(8,128)}) custom-call(bf16[1,1,2,64,4096]{4,3,2,1,0:T(8,128)(2,1)S(1)} %get-tuple-element.8.refs_0_, bf16[1,1,2,64,4096]{4,3,2,1,0:T(8,128)(2,1)S(1)} %get-tuple-element.9.refs_1_, ...), custom_call_target="tpu_custom_call" | custom-call | tf_op jit(solution)/shard_map/pallas_call | solution.py:655

commit v3 on v2

--- a/solution.py
+++ b/solution.py
@@ -93,26 +93,33 @@
     team = 2 * x_count
     place = core * x_count + x
 
-    def member(k):
-        index = lax.rem(place + k, team)
-        return index, (lax.div(index, x_count), seq - x + lax.rem(index, x_count))
-
-    def along_y(k):
-        index = lax.rem(y + k, y_count)
+    def member(k, back=False):
+        steps = k % x_count
+        here_x = lax.rem(x + (x_count - steps if back else steps), x_count)
+        here_core = core if k < x_count else other
+        return here_core * x_count + here_x, (here_core, seq - x + here_x)
+
+    def along_y(k, back=False):
+        index = lax.rem(y + (y_count - k if back else k), y_count)
         return index, (core, seq + (index - y) * x_count)
 
-    def along_z(k):
-        index = lax.rem(z + k, z_count)
+    def along_z(k, back=False):
+        index = lax.rem(z + (z_count - k if back else k), z_count)
         return index, (core, seq + (index - z) * (x_count * y_count))
+
+    def order(ring, count):
+        around = x_count if ring is member else count
+        return sorted(range(1, count), key=lambda k: -min(k % around, -k % around))
 
     def columns(c):
         return pl.ds(pl.multiple_of(c * width, width), width)
 
     barrier = pltpu.get_barrier_semaphore()
-    partners = [sibling, following, previous]
-    partners += [member(k)[1] for k in range(1, team)]
-    partners += [along_y(k)[1] for k in range(1, y_count)]
-    partners += [along_z(k)[1] for k in range(1, z_count)]
+    partners = [along_z(k)[1] for k in order(along_z, z_count)]
+    partners += [following, previous]
+    partners += [along_y(k)[1] for k in order(along_y, y_count)]
+    partners += [member(k)[1] for k in order(member, team)]
+    partners += [sibling]
     for partner in partners:
         pl.semaphore_signal(barrier, inc=1, device_id=partner, device_id_type=MESH)
 
@@ -232,14 +239,25 @@
             device_id_type=MESH,
         )
 
-    def halos(c):
-        halo_mix(c).start()
-        halo_gg(chunks - 1 - c).start()
+    mix_turns = (x == x_count - 1) & (y == y_count - 1)
+    gg_turns = (x == 0) & (y == 0)
+
+    def halos(first, last, turning):
+        @pl.when(mix_turns == turning)
+        def _():
+            for c in range(first, last):
+                halo_mix(c).start()
+
+        @pl.when(gg_turns == turning)
+        def _():
+            for c in range(first, last):
+                halo_gg(chunks - 1 - c).start()
 
     def lanes_of(c, q):
         return pl.ds(pl.multiple_of(c * width + q * LANES, LANES), LANES)
 
-    early = 3 * chunks // 4
+    plain = (3 * chunks // 4, 7 * chunks // 8, chunks, chunks)
+    turned = (3 * chunks // 4, 7 * chunks // 8, 7 * chunks // 8, chunks)
 
     def assemble(c, carry):
         back = chunks - 1 - c
@@ -259,7 +277,7 @@
             )
             mixx[c * per_chunk + q, rows:, :] = in_order(mine, received).astype(jnp.bfloat16)
 
-        @pl.when(c < early)
+        @pl.when(c < jnp.where(mix_turns, turned[0], plain[0]))
         def _():
             halo_mix(c).start()
 
@@ -274,7 +292,7 @@
                 gate * cot[:, here].astype(jnp.float32)
             ).astype(jnp.bfloat16)
 
-        @pl.when(c < early)
+        @pl.when(c < jnp.where(gg_turns, turned[0], plain[0]))
         def _():
             halo_gg(back).start()
 
@@ -454,7 +472,7 @@
 
     def exchange(ring, count, here, buffer, source, send, recv):
         copies = []
-        for k in range(1, count):
+        for k in order(ring, count):
             index, device = ring(k)
             copy = remote(
                 source(index), buffer.at[here], send.at[k - 1], recv.at[k - 1], device
@@ -465,7 +483,7 @@
 
     def arrive(ring, count, buffer, send, recv):
         for k in range(1, count):
-            index, device = ring(count - k)
+            index, device = ring(k, back=True)
             remote(
                 buffer.at[index], buffer.at[index], send.at[k - 1], recv.at[k - 1], device
             ).wait_recv()
@@ -509,7 +527,7 @@
             diag[piece_rows(place), :] = total_of(buffer, count) * scale
             own_piece.start()
             copies = []
-            for k in range(1, team):
+            for k in order(member, team):
                 index, device = member(k)
                 copy = remote(
                     diag.at[piece_rows(place)],
@@ -522,7 +540,7 @@
                 copies.append(copy)
             return copies
         for k in range(1, team):
-            index, device = member(team - k)
+            index, device = member(k, back=True)
             remote(
                 gf_hbm.at[piece_rows(index)],
                 gf_hbm.at[piece_rows(index)],
@@ -532,18 +550,6 @@
             ).wait_recv()
         return []
 
-    middle_chunk = (early + chunks) // 2
-    late = [early, middle_chunk, middle_chunk, chunks]
-    ends = [before, chunks // 2, 5 * chunks // 8, 7 * chunks // 8, chunks]
-    for stage in range(4):
-        if stage < 3:
-            for c in range(late[stage], late[stage + 1]):
-                halos(c)
-        lax.fori_loop(ends[stage], ends[stage + 1], step, 0)
-        sent += advance(stage)
-
-    for copy in sent:
-        copy.wait_send()
 
     def finish(c, carry):
         halo_mix(c).wait_send()
@@ -554,7 +560,19 @@
             back_copy(which, c).wait()
         return carry
 
-    lax.fori_loop(0, chunks, finish, 0)
+    ends = (before, chunks // 2, 5 * chunks // 8, 7 * chunks // 8, chunks)
+    for stage in range(4):
+        if stage < 3:
+            halos(plain[stage], plain[stage + 1], False)
+            halos(turned[stage], turned[stage + 1], True)
+        lax.fori_loop(ends[stage], ends[stage + 1], step, 0)
+        if stage == 3:
+            for copy in sent[: -(team - 1)]:
+                copy.wait_send()
+            lax.fori_loop(0, chunks, finish, 0)
+        sent += advance(stage)
+    for copy in sent[-(team - 1) :]:
+        copy.wait_send()
     own_piece.wait()
 
 

time: 51.3 us -> 50.8 us (level)
    pallas_call x1, Pallas kernels: 48.9 us -> 48.4 us  [body(): pl.pallas_call(functools.partial(kernel_body, dims, chunks, 1.0 / math.sq...]
where the time goes in v3:
time: 50.8 us; the launch traced here: 50.7 us
  Pallas kernels  50.1 us (99%)
  between operations  0.64 us (1%)
    pallas_call x1, Pallas kernels, body(): pl.pallas_call(functools.partial(kernel_body, dims, chunks, 1.0 / math.sq...  48.4 us
    pallas_call x1, Pallas kernels, body(): pl.pallas_call(functools.partial(hand_over, count), out_shape=tuple((jax....  1.74 us

profile of v3, /device:TPU:1, one launch (start us, length us, event | category | flops | bytes accessed | tf_op | source)
XLA Modules:
  0.0 50.7 jit_solution(17956439274232388840)
XLA Ops:
  0.6 48.4 %shard_map.102 = (bf16[1,1,2,64,4096]{4,3,2,1,0:T(8,128)(2,1)S(1)}, bf16[1,1,2,64,4096]{4,3,2,1,0:T(8,128)(2,1)S(1)}, bf16[1,1,2,64,4096]{4,3,2,1,0:T(8,128)(2,1)S(1)}, f32[128,128]{1,0:T(8,128)S(1)}) custom-call(bf16[1,1,2,64,4096]{4,3,2,1,0:T(8,128)(2,1)} %query_hbm.1, bf16[1,1,2,64,4096]{4,3,2,1,0:T(8,128)(2,1)} %key_hbm.1, ...), custom_call_target="tpu_custom_call" | custom-call | flops 805306368 | bytes 7340032 | tf_op jit(solution)/shard_map/pallas_call | solution.py:612
  49.0 1.7 %shard_map.103 = (bf16[1,1,2,64,4096]{4,3,2,1,0:T(8,128)(2,1)}, bf16[1,1,2,64,4096]{4,3,2,1,0:T(8,128)(2,1)}, bf16[1,1,2,64,4096]{4,3,2,1,0:T(8,128)(2,1)}, f32[128,128]{1,0:T(8,128)}) custom-call(bf16[1,1,2,64,4096]{4,3,2,1,0:T(8,128)(2,1)S(1)} %get-tuple-element.8.refs_0_, bf16[1,1,2,64,4096]{4,3,2,1,0:T(8,128)(2,1)S(1)} %get-tuple-element.9.refs_1_, ...), custom_call_target="tpu_custom_call" | custom-call | tf_op jit(solution)/shard_map/pallas_call | solution.py:673

commit v4 on v3

--- a/solution.py
+++ b/solution.py
@@ -48,7 +48,6 @@
     stage_oth,
     piece_one,
     piece_two,
-    piece_three,
     small_sem,
     own_sem,
     swap_send,
@@ -64,8 +63,6 @@
     one_recv,
     two_send,
     two_recv,
-    three_send,
-    three_recv,
     four_send,
     four_recv,
     final_sem,
@@ -90,34 +87,44 @@
     sibling = (other, seq)
     following = (core, lax.rem(seq + 1, seq_count))
     previous = (core, lax.rem(seq + seq_count - 1, seq_count))
-    team = 2 * x_count
-    place = core * x_count + x
+    y_low, y_high = lax.rem(y, 2), lax.div(y, 2)
+    pairs = y_count // 2
+    team = 4 * x_count
+    place = (core * 2 + y_low) * x_count + x
+    across_count = pairs * z_count
+    across_place = y_high * z_count + z
 
     def member(k, back=False):
         steps = k % x_count
         here_x = lax.rem(x + (x_count - steps if back else steps), x_count)
-        here_core = core if k < x_count else other
-        return here_core * x_count + here_x, (here_core, seq - x + here_x)
-
-    def along_y(k, back=False):
-        index = lax.rem(y + (y_count - k if back else k), y_count)
-        return index, (core, seq + (index - y) * x_count)
-
-    def along_z(k, back=False):
-        index = lax.rem(z + (z_count - k if back else k), z_count)
-        return index, (core, seq + (index - z) * (x_count * y_count))
+        here_low = lax.rem(y_low + (k // x_count) % 2, 2)
+        here_core = core if k < 2 * x_count else other
+        index = (here_core * 2 + here_low) * x_count + here_x
+        return index, (here_core, seq + (here_x - x) + (here_low - y_low) * x_count)
+
+    def across(k, back=False):
+        steps, turns = k % z_count, k // z_count
+        here_z = lax.rem(z + (z_count - steps if back else steps), z_count)
+        here_high = lax.rem(y_high + (pairs - turns if back else turns), pairs)
+        apart = (here_z - z) * (x_count * y_count) + (here_high - y_high) * (2 * x_count)
+        return here_high * z_count + here_z, (core, seq + apart)
+
+    def hops(ring, k):
+        if ring is member:
+            steps = k % x_count
+            return min(steps, x_count - steps) + (k // x_count) % 2
+        steps = k % z_count
+        return min(steps, z_count - steps) + 2 * (k // z_count)
 
     def order(ring, count):
-        around = x_count if ring is member else count
-        return sorted(range(1, count), key=lambda k: -min(k % around, -k % around))
+        return sorted(range(1, count), key=lambda k: -hops(ring, k))
 
     def columns(c):
         return pl.ds(pl.multiple_of(c * width, width), width)
 
     barrier = pltpu.get_barrier_semaphore()
-    partners = [along_z(k)[1] for k in order(along_z, z_count)]
+    partners = [across(k)[1] for k in order(across, across_count)]
     partners += [following, previous]
-    partners += [along_y(k)[1] for k in order(along_y, y_count)]
     partners += [member(k)[1] for k in order(member, team)]
     partners += [sibling]
     for partner in partners:
@@ -256,8 +263,8 @@
     def lanes_of(c, q):
         return pl.ds(pl.multiple_of(c * width + q * LANES, LANES), LANES)
 
-    plain = (3 * chunks // 4, 7 * chunks // 8, chunks, chunks)
-    turned = (3 * chunks // 4, 7 * chunks // 8, 7 * chunks // 8, chunks)
+    plain = (3 * chunks // 4, 7 * chunks // 8, chunks)
+    turned = (3 * chunks // 4, 7 * chunks // 8, chunks)
 
     def assemble(c, carry):
         back = chunks - 1 - c
@@ -503,28 +510,22 @@
         member, team, place, piece_one, lambda i: terms.at[piece_rows(i)], one_send, one_recv
     )
 
-    middle = (
-        (along_z, z_count, z, piece_three, three_send, three_recv),
-        (along_y, y_count, y, piece_two, two_send, two_recv),
-    )
-
     def advance(stage):
         if stage == 0:
             arrive(member, team, piece_one, one_send, one_recv)
-            ring, count, here, buffer, send, recv = middle[0]
-            buffer[here] = total_of(piece_one, team)
-            return exchange(ring, count, here, buffer, lambda i: buffer.at[here], send, recv)
+            piece_two[across_place] = total_of(piece_one, team)
+            return exchange(
+                across,
+                across_count,
+                across_place,
+                piece_two,
+                lambda i: piece_two.at[across_place],
+                two_send,
+                two_recv,
+            )
         if stage == 1:
-            ring, count, here, buffer, send, recv = middle[0]
-            arrive(ring, count, buffer, send, recv)
-            total = total_of(buffer, count)
-            ring, count, here, buffer, send, recv = middle[1]
-            buffer[here] = total
-            return exchange(ring, count, here, buffer, lambda i: buffer.at[here], send, recv)
-        if stage == 2:
-            ring, count, here, buffer, send, recv = middle[1]
-            arrive(ring, count, buffer, send, recv)
-            diag[piece_rows(place), :] = total_of(buffer, count) * scale
+            arrive(across, across_count, piece_two, two_send, two_recv)
+            diag[piece_rows(place), :] = total_of(piece_two, across_count) * scale
             own_piece.start()
             copies = []
             for k in order(member, team):
@@ -560,13 +561,13 @@
             back_copy(which, c).wait()
         return carry
 
-    ends = (before, chunks // 2, 5 * chunks // 8, 7 * chunks // 8, chunks)
-    for stage in range(4):
-        if stage < 3:
+    ends = (before, chunks // 2, 7 * chunks // 8, chunks)
+    for stage in range(3):
+        if stage < 2:
             halos(plain[stage], plain[stage + 1], False)
             halos(turned[stage], turned[stage + 1], True)
         lax.fori_loop(ends[stage], ends[stage + 1], step, 0)
-        if stage == 3:
+        if stage == 2:
             for copy in sent[: -(team - 1)]:
                 copy.wait_send()
             lax.fori_loop(0, chunks, finish, 0)
@@ -601,7 +602,8 @@
     rows = cotangent.shape[1]
     groups = filters.shape[0]
     z_count, y_count, x_count = dims
-    team = 2 * x_count
+    team = 4 * x_count
+    across_count = y_count // 2 * z_count
     piece = groups // team
     width = features // chunks
     tiles = features // LANES
@@ -639,8 +641,7 @@
             pltpu.VMEM((3, chunks, slot, width), half),
             pltpu.VMEM((3, chunks, slot, width), half),
             pltpu.VMEM((team, piece, rows), single),
-            pltpu.VMEM((y_count, piece, rows), single),
-            pltpu.VMEM((z_count, piece, rows), single),
+            pltpu.VMEM((across_count, piece, rows), single),
             dma((3,)),
             dma((4,)),
             dma((3, chunks)),
@@ -654,10 +655,8 @@
             dma((3, chunks)),
             dma((team - 1,)),
             dma((team - 1,)),
-            dma((y_count - 1,)),
-            dma((y_count - 1,)),
-            dma((z_count - 1,)),
-            dma((z_count - 1,)),
+            dma((across_count - 1,)),
+            dma((across_count - 1,)),
             dma((team - 1,)),
             dma((team - 1,)),
             dma,

time: 50.8 us -> 50.4 us (level)
  no operation moved by 1% of the time
where the time goes in v4:
time: 50.4 us; the launch traced here: 50.3 us
  Pallas kernels  49.7 us (99%)
  between operations  0.64 us (1%)
    pallas_call x1, Pallas kernels, body(): pl.pallas_call(functools.partial(kernel_body, dims, chunks, 1.0 / math.sq...  48 us
    pallas_call x1, Pallas kernels, body(): pl.pallas_call(functools.partial(hand_over, count), out_shape=tuple((jax....  1.74 us

profile of v4, /device:TPU:1, one launch (start us, length us, event | category | flops | bytes accessed | tf_op | source)
XLA Modules:
  0.0 50.3 jit_solution(4585562760697485725)
XLA Ops:
  0.6 48.0 %shard_map.102 = (bf16[1,1,2,64,4096]{4,3,2,1,0:T(8,128)(2,1)S(1)}, bf16[1,1,2,64,4096]{4,3,2,1,0:T(8,128)(2,1)S(1)}, bf16[1,1,2,64,4096]{4,3,2,1,0:T(8,128)(2,1)S(1)}, f32[128,128]{1,0:T(8,128)S(1)}) custom-call(bf16[1,1,2,64,4096]{4,3,2,1,0:T(8,128)(2,1)} %query_hbm.1, bf16[1,1,2,64,4096]{4,3,2,1,0:T(8,128)(2,1)} %key_hbm.1, ...), custom_call_target="tpu_custom_call" | custom-call | flops 805306368 | bytes 7340032 | tf_op jit(solution)/shard_map/pallas_call | solution.py:614
  48.6 1.7 %shard_map.103 = (bf16[1,1,2,64,4096]{4,3,2,1,0:T(8,128)(2,1)}, bf16[1,1,2,64,4096]{4,3,2,1,0:T(8,128)(2,1)}, bf16[1,1,2,64,4096]{4,3,2,1,0:T(8,128)(2,1)}, f32[128,128]{1,0:T(8,128)}) custom-call(bf16[1,1,2,64,4096]{4,3,2,1,0:T(8,128)(2,1)S(1)} %get-tuple-element.8.refs_0_, bf16[1,1,2,64,4096]{4,3,2,1,0:T(8,128)(2,1)S(1)} %get-tuple-element.9.refs_1_, ...), custom_call_target="tpu_custom_call" | custom-call | tf_op jit(solution)/shard_map/pallas_call | solution.py:672
